TPU v7x, 32 devices: a whole 2x2x4 slice. The times are simulated.
32 devices in a mesh: wide: 16 (over z, y, x), narrow: 2 (over core).
Axes of the slice: x: 2, y: 2, z: 4, core: 2. Of those that a mesh axis runs over, the one named last changes fastest.
Arguments:
- amplitudes: bfloat16 [256, 256, 128], P('wide', 'narrow'), may hold values from -6 to 6
- send_list: int32 [16, 32], P('wide'), may hold values from 0 to 15
- tile_positions: int32 [128, 16], P('wide', 'narrow'), may hold values from 0 to 31
- integrals: bfloat16 [128, 16, 128, 128], P('wide', 'narrow'), may hold values from -0.125 to 0.125
Outputs:
- ladder: bfloat16 [128, 256, 128], P('wide', 'narrow')
All inputs are finite; a program needn't handle non-finite values.
Results may differ from a plain program's by a relative error of at most 0.001.
Values may be sent and summed in bfloat16 or wider, within the bound.
No kernel may reach another device: no remote copies, remote signals or barrier semaphores. Data moves between devices by JAX's collectives and lax.ppermute only.
A program may use at most 64 MiB of HBM per device.

v0:
```python
import functools

import jax
import jax.numpy as jnp
from jax import lax
from jax.experimental import pallas as pl
from jax.experimental.pallas import tpu as pltpu
from jax.sharding import PartitionSpec as P

VMEM_LIMIT = 48 * 1024 * 1024
PICK_GRANT = 62 * 1024 * 1024


def pick_outgoing(send_ref, amplitudes_ref, out_ref, sends, held, in_sems, sems):
    fetch_sends = pltpu.make_async_copy(send_ref, sends, in_sems.at[0])
    fetch_tiles = pltpu.make_async_copy(amplitudes_ref, held, in_sems.at[1])
    fetch_tiles.start()
    fetch_sends.start()
    fetch_sends.wait()
    fetch_tiles.wait()
    copies = []
    for slot in range(out_ref.shape[0]):
        copy = pltpu.make_async_copy(
            held.at[sends[0, slot]], out_ref.at[slot], sems.at[slot]
        )
        copy.start()
        copies.append(copy)
    for copy in copies:
        copy.wait()


def contract(count, *refs):
    places = refs[:count]
    received_ref = refs[count]
    blocks = list(refs[count + 1 : 2 * count + 1])
    out_ref, stage, out_sems, held, in_sems = refs[2 * count + 1 :]
    tiles, per_block, inner, columns = blocks[0].shape
    fetches = [pltpu.make_async_copy(blocks[-1].at[x], held.at[x], in_sems.at[x]) for x in range(tiles)]
    for fetch in fetches:
        fetch.start()
    blocks[-1] = held
    copies = []
    for x in range(tiles):
        total = None
        for number, (place_ref, block_ref) in enumerate(zip(places, blocks)):
            picked = jnp.concatenate(
                [received_ref[place_ref[x, k]] for k in range(per_block)], axis=1
            )
            if number == count - 1:
                fetches[x].wait()
            part = jnp.dot(
                picked,
                block_ref[x].reshape(per_block * inner, columns),
                preferred_element_type=jnp.float32,
            )
            total = part if total is None else total + part
        stage[x] = total.astype(stage.dtype)
        copy = pltpu.make_async_copy(stage.at[x], out_ref.at[x], out_sems.at[x])
        copy.start()
        copies.append(copy)
    for copy in copies:
        copy.wait()


def on_device(narrow, amplitudes, send_list, tile_positions, integrals):
    smem = pl.BlockSpec(memory_space=pltpu.SMEM)
    anywhere = pl.BlockSpec(memory_space=pl.ANY)
    vmem = pl.BlockSpec(memory_space=pltpu.VMEM)
    params = pltpu.CompilerParams(vmem_limit_bytes=VMEM_LIMIT)
    slots = send_list.shape[1]
    tile_bytes = amplitudes.shape[1] * amplitudes.shape[2] * 2
    outgoing = pl.pallas_call(
        pick_outgoing,
        out_shape=jax.ShapeDtypeStruct((slots,) + amplitudes.shape[1:], amplitudes.dtype),
        in_specs=[anywhere, anywhere],
        out_specs=anywhere,
        scratch_shapes=[
            pltpu.SMEM(send_list.shape, send_list.dtype),
            pltpu.VMEM(amplitudes.shape, amplitudes.dtype),
            pltpu.SemaphoreType.DMA((2,)),
            pltpu.SemaphoreType.DMA((slots,)),
        ],
        compiler_params=pltpu.CompilerParams(vmem_limit_bytes=PICK_GRANT),
        cost_estimate=pl.CostEstimate(flops=0, bytes_accessed=2 * slots * tile_bytes, transcendentals=0),
    )(send_list, amplitudes)
    if narrow == 2:
        swap = [(0, 1), (1, 0)]
        places = [tile_positions, lax.ppermute(tile_positions, "narrow", swap)]
        blocks = [integrals, lax.ppermute(integrals, "narrow", swap)]
    else:
        places = [lax.all_gather(tile_positions, "narrow", axis=1, tiled=True)]
        blocks = [lax.all_gather(integrals, "narrow", axis=1, tiled=True)]
    received = lax.all_to_all(outgoing, "wide", split_axis=0, concat_axis=0, tiled=True)
    tiles, pairs, columns = integrals.shape[0], amplitudes.shape[1], integrals.shape[3]
    count = len(blocks)
    return pl.pallas_call(
        functools.partial(contract, count),
        out_shape=jax.ShapeDtypeStruct((tiles, pairs, columns), jnp.bfloat16),
        in_specs=[smem] * count + [vmem] * count + [anywhere],
        out_specs=pl.BlockSpec(memory_space=pl.ANY),
        scratch_shapes=[
            pltpu.VMEM((tiles, pairs, columns), jnp.bfloat16),
            pltpu.SemaphoreType.DMA((tiles,)),
            pltpu.VMEM(blocks[-1].shape, blocks[-1].dtype),
            pltpu.SemaphoreType.DMA((tiles,)),
        ],
        compiler_params=params,
    )(*places, received, *blocks)


def solution(mesh):
    placed = (
        P("wide", "narrow", None),
        P("wide", None),
        P("wide", "narrow"),
        P("wide", "narrow", None, None),
    )
    return jax.shard_map(
        functools.partial(on_device, mesh.shape["narrow"]),
        mesh=mesh,
        in_specs=placed,
        out_specs=P("wide", "narrow", None),
        check_vma=False,
    )
```

profile of v0, /device:TPU:0, one launch (start us, length us, event | category | flops | bytes accessed | tf_op | source)
XLA Modules:
  0.0 40.8 jit_solution(13902193729664752028)
XLA Ops:
  0.0 0.0 copy-start.1
  0.0 0.5 %collective-permute-start.1 = (bf16[8,8,128,128]{3,2,1,0:T(8,128)(2,1)}, bf16[8,8,128,128]{3,2,1,0:T(8,128)(2,1)}, u32[]{:S(2)}, u32[]{:S(2)}) collective-permute-start(bf16[8,8,128,128]{3,2,1,0:T(8,128)(2,1)} %refs_3_.1), channel_id=1, source_target_pairs={{0,1},{1,0},{2,3},{3,2},{4,5},{5,4},{6,7},{7,6},{8,9},{9,8},{10,11... | collective-permute-start | bytes 6291464 | tf_op jit(solution)/shard_map/ppermute | solution.py:89
  0.5 2.3 %shard_map.46 = bf16[32,128,128]{2,1,0:T(8,128)(2,1)} custom-call(s32[1,32]{1,0:T(1,128)} %send_ref.1, bf16[16,128,128]{2,1,0:T(8,128)(2,1)} %amplitudes_ref.1), custom_call_target="tpu_custom_call" | custom-call | bytes 2097152 | tf_op jit(solution)/shard_map/pallas_call | solution.py:72
  2.8 0.0 copy-start
  2.8 8.0 %all-to-all-start = ((bf16[32,128,128]{2,1,0:T(8,128)(2,1)}), bf16[32,128,128]{2,1,0:T(8,128)(2,1)S(1)}, u32[]{:S(2)}, u32[]{:S(2)}) async-start(bf16[32,128,128]{2,1,0:T(8,128)(2,1)} %shard_map.46), calls=%async_computation | async-start | bytes 2097152 | tf_op jit(solution)/shard_map/all_to_all | solution.py:93
  10.8 0.0 copy-done.1
  10.8 0.3 collective-permute-start
  11.1 0.9 %collective-permute-done.refs_1_ = s32[8,8]{1,0:T(8,128)S(1)} collective-permute-done((s32[8,8]{1,0:T(8,128)S(1)}, s32[8,8]{1,0:T(8,128)S(1)}, u32[]{:S(2)}, u32[]{:S(2)}) %collective-permute-start) | collective-permute-done | bytes 288 | tf_op jit(solution)/shard_map/ppermute | solution.py:88
  12.1 23.6 %all-to-all-done.refs_2_ = bf16[32,128,128]{2,1,0:T(8,128)(2,1)S(1)} async-done(((bf16[32,128,128]{2,1,0:T(8,128)(2,1)}), bf16[32,128,128]{2,1,0:T(8,128)(2,1)S(1)}, u32[]{:S(2)}, u32[]{:S(2)}) %all-to-all-start) | async-done | bytes 1048608 | tf_op jit(solution)/shard_map/all_to_all | solution.py:93
  35.6 0.0 collective-permute-done.1.refs_4_
  35.6 0.0 copy-done
  35.7 5.2 %shard_map.47 = bf16[8,128,128]{2,1,0:T(8,128)(2,1)} custom-call(s32[8,8]{1,0:T(8,128)S(1)} %copy-done.1, s32[8,8]{1,0:T(8,128)S(1)} %collective-permute-done.refs_1_, bf16[32,128,128]{2,1,0:T(8,128)(2,1)S(1)} %all-to-all-done.refs_2_, bf16[8,8,128,128]{3,2,1,0:T(8,128)(2,1)S(1)} %copy-done, bf16[8,8,128,128]{3,2,1,0:T(8,128)(2,1)} %collective-permute-done.1.refs_4_), custom_call_target="tpu_custom_call" | custom-call | tf_op jit(solution)/shard_map/pallas_call | solution.py:96
Async XLA Ops:
  0.0 10.8 %copy-start.1 = (s32[8,8]{1,0:T(8,128)S(1)}, s32[8,8]{1,0:T(8,128)}, u32[]{:S(2)}) copy-start(s32[8,8]{1,0:T(8,128)} %refs_0_.1) | copy-start | bytes 772
  0.0 35.6 %collective-permute-start.1 = (bf16[8,8,128,128]{3,2,1,0:T(8,128)(2,1)}, bf16[8,8,128,128]{3,2,1,0:T(8,128)(2,1)}, u32[]{:S(2)}, u32[]{:S(2)}) collective-permute-start(bf16[8,8,128,128]{3,2,1,0:T(8,128)(2,1)} %refs_3_.1), channel_id=1, source_target_pairs={{0,1},{1,0},{2,3},{3,2},{4,5},{5,4},{6,7},{7,6},{8,9},{9,8},{10,11... | collective-permute-start | bytes 6291464 | tf_op jit(solution)/shard_map/ppermute | solution.py:89
  2.8 32.9 %copy-start = (bf16[8,8,128,128]{3,2,1,0:T(8,128)(2,1)S(1)}, bf16[8,8,128,128]{3,2,1,0:T(8,128)(2,1)}, u32[]{:S(2)}) copy-start(bf16[8,8,128,128]{3,2,1,0:T(8,128)(2,1)} %refs_3_.1) | copy-start | bytes 6291460
  2.8 32.8 %all-to-all-start = ((bf16[32,128,128]{2,1,0:T(8,128)(2,1)}), bf16[32,128,128]{2,1,0:T(8,128)(2,1)S(1)}, u32[]{:S(2)}, u32[]{:S(2)}) async-start(bf16[32,128,128]{2,1,0:T(8,128)(2,1)} %shard_map.46), calls=%async_computation | async-start | bytes 2097152 | tf_op jit(solution)/shard_map/all_to_all | solution.py:93
  10.8 1.2 %collective-permute-start = (s32[8,8]{1,0:T(8,128)S(1)}, s32[8,8]{1,0:T(8,128)S(1)}, u32[]{:S(2)}, u32[]{:S(2)}) collective-permute-start(s32[8,8]{1,0:T(8,128)S(1)} %copy-done.1), channel_id=1, source_target_pairs={{0,1},{1,0},{2,3},{3,2},{4,5},{5,4},{6,7},{7,6},{8,9},{9,8},{10,11... | collective-permute-start | bytes 776 | tf_op jit(solution)/shard_map/ppermute | solution.py:88
where the time goes:
time: 41.4 us; the launch traced here: 40.8 us
  waiting for transfers between devices  24.5 us (59%)
  starting transfers between devices  8.75 us (21%)
  Pallas kernels  7.49 us (18%)
    all_to_all x1, waiting for transfers between devices, on_device(): lax.all_to_all(outgoing, 'wide', split_axis=0, concat_axis=0, tiled=True)  23.6 us
    all_to_all x1, starting transfers between devices, on_device(): lax.all_to_all(outgoing, 'wide', split_axis=0, concat_axis=0, tiled=True)  8.02 us
    pallas_call x1, Pallas kernels, on_device(): pl.pallas_call(functools.partial(contract, count), out_shape=jax.ShapeDty...  5.16 us
    pallas_call x1, Pallas kernels, on_device(): pl.pallas_call(pick_outgoing, out_shape=jax.ShapeDtypeStruct((slots,) + a...  2.33 us
    ppermute x1, waiting for transfers between devices, on_device(): places = [tile_positions, lax.ppermute(tile_positions, 'narrow', swap)]  0.95 us
  transfers between devices with their start and end apart: 3, of which 2 were waited for; matrix products, arithmetic and copies ran while one was open for 0% of the time, Pallas kernels for 6%

commit v1 on v0

--- a/solution.py
+++ b/solution.py
@@ -33,33 +33,33 @@
     places = refs[:count]
     received_ref = refs[count]
     blocks = list(refs[count + 1 : 2 * count + 1])
-    out_ref, stage, out_sems, held, in_sems = refs[2 * count + 1 :]
+    out_ref, totals, stage, held, in_sem, out_sem = refs[2 * count + 1 :]
     tiles, per_block, inner, columns = blocks[0].shape
-    fetches = [pltpu.make_async_copy(blocks[-1].at[x], held.at[x], in_sems.at[x]) for x in range(tiles)]
-    for fetch in fetches:
-        fetch.start()
+    fetch = pltpu.make_async_copy(blocks[-1], held, in_sem)
+    fetch.start()
     blocks[-1] = held
     copies = []
-    for x in range(tiles):
-        total = None
-        for number, (place_ref, block_ref) in enumerate(zip(places, blocks)):
+    for number, (place_ref, block_ref) in enumerate(zip(places, blocks)):
+        if number == count - 1:
+            fetch.wait()
+        for x in range(tiles):
             picked = jnp.concatenate(
                 [received_ref[place_ref[x, k]] for k in range(per_block)], axis=1
             )
-            if number == count - 1:
-                fetches[x].wait()
             part = jnp.dot(
                 picked,
                 block_ref[x].reshape(per_block * inner, columns),
                 preferred_element_type=jnp.float32,
             )
-            total = part if total is None else total + part
-        stage[x] = total.astype(stage.dtype)
-        copy = pltpu.make_async_copy(stage.at[x], out_ref.at[x], out_sems.at[x])
-        copy.start()
-        copies.append(copy)
-    for copy in copies:
-        copy.wait()
+            if number:
+                part = totals[x] + part
+            if number < count - 1:
+                totals[x] = part
+            else:
+                stage[x] = part.astype(stage.dtype)
+    copy = pltpu.make_async_copy(stage, out_ref, out_sem)
+    copy.start()
+    copy.wait()
 
 
 def on_device(narrow, amplitudes, send_list, tile_positions, integrals):
@@ -99,10 +99,11 @@
         in_specs=[smem] * count + [vmem] * count + [anywhere],
         out_specs=pl.BlockSpec(memory_space=pl.ANY),
         scratch_shapes=[
+            pltpu.VMEM((tiles, pairs, columns), jnp.float32),
             pltpu.VMEM((tiles, pairs, columns), jnp.bfloat16),
-            pltpu.SemaphoreType.DMA((tiles,)),
             pltpu.VMEM(blocks[-1].shape, blocks[-1].dtype),
-            pltpu.SemaphoreType.DMA((tiles,)),
+            pltpu.SemaphoreType.DMA,
+            pltpu.SemaphoreType.DMA,
         ],
         compiler_params=params,
     )(*places, received, *blocks)

time: 41.4 us -> 40.5 us (0.978)
  Pallas kernels: 7.49 us -> 6.54 us
    pallas_call x1, Pallas kernels: 5.16 us -> 4.21 us  [on_device(): pl.pallas_call(functools.partial(contract, count), out_shape=jax.ShapeDty...]
where the time goes in v1:
time: 40.5 us; the launch traced here: 39.9 us
  waiting for transfers between devices  24.5 us (60%)
  starting transfers between devices  8.75 us (22%)
  Pallas kernels  6.54 us (16%)
    all_to_all x1, waiting for transfers between devices, on_device(): lax.all_to_all(outgoing, 'wide', split_axis=0, concat_axis=0, tiled=True)  23.6 us
    all_to_all x1, starting transfers between devices, on_device(): lax.all_to_all(outgoing, 'wide', split_axis=0, concat_axis=0, tiled=True)  8.02 us
    pallas_call x1, Pallas kernels, on_device(): pl.pallas_call(functools.partial(contract, count), out_shape=jax.ShapeDty...  4.21 us
    pallas_call x1, Pallas kernels, on_device(): pl.pallas_call(pick_outgoing, out_shape=jax.ShapeDtypeStruct((slots,) + a...  2.33 us
    ppermute x1, waiting for transfers between devices, on_device(): places = [tile_positions, lax.ppermute(tile_positions, 'narrow', swap)]  0.95 us
  transfers between devices with their start and end apart: 3, of which 2 were waited for; matrix products, arithmetic and copies ran while one was open for 0% of the time, Pallas kernels for 6%

profile of v1, /device:TPU:0, one launch (start us, length us, event | category | flops | bytes accessed | tf_op | source)
XLA Modules:
  0.0 39.9 jit_solution(7612914755025381514)
XLA Ops:
  0.0 0.0 copy-start.1
  0.0 0.5 %collective-permute-start.1 = (bf16[8,8,128,128]{3,2,1,0:T(8,128)(2,1)}, bf16[8,8,128,128]{3,2,1,0:T(8,128)(2,1)}, u32[]{:S(2)}, u32[]{:S(2)}) collective-permute-start(bf16[8,8,128,128]{3,2,1,0:T(8,128)(2,1)} %refs_3_.1), channel_id=1, source_target_pairs={{0,1},{1,0},{2,3},{3,2},{4,5},{5,4},{6,7},{7,6},{8,9},{9,8},{10,11... | collective-permute-start | bytes 6291464 | tf_op jit(solution)/shard_map/ppermute | solution.py:89
  0.5 2.3 %shard_map.46 = bf16[32,128,128]{2,1,0:T(8,128)(2,1)} custom-call(s32[1,32]{1,0:T(1,128)} %send_ref.1, bf16[16,128,128]{2,1,0:T(8,128)(2,1)} %amplitudes_ref.1), custom_call_target="tpu_custom_call" | custom-call | bytes 2097152 | tf_op jit(solution)/shard_map/pallas_call | solution.py:72
  2.8 0.0 copy-start
  2.8 8.0 %all-to-all-start = ((bf16[32,128,128]{2,1,0:T(8,128)(2,1)}), bf16[32,128,128]{2,1,0:T(8,128)(2,1)S(1)}, u32[]{:S(2)}, u32[]{:S(2)}) async-start(bf16[32,128,128]{2,1,0:T(8,128)(2,1)} %shard_map.46), calls=%async_computation | async-start | bytes 2097152 | tf_op jit(solution)/shard_map/all_to_all | solution.py:93
  10.8 0.0 copy-done.1
  10.8 0.3 collective-permute-start
  11.1 0.9 %collective-permute-done.refs_1_ = s32[8,8]{1,0:T(8,128)S(1)} collective-permute-done((s32[8,8]{1,0:T(8,128)S(1)}, s32[8,8]{1,0:T(8,128)S(1)}, u32[]{:S(2)}, u32[]{:S(2)}) %collective-permute-start) | collective-permute-done | bytes 288 | tf_op jit(solution)/shard_map/ppermute | solution.py:88
  12.1 23.6 %all-to-all-done.refs_2_ = bf16[32,128,128]{2,1,0:T(8,128)(2,1)S(1)} async-done(((bf16[32,128,128]{2,1,0:T(8,128)(2,1)}), bf16[32,128,128]{2,1,0:T(8,128)(2,1)S(1)}, u32[]{:S(2)}, u32[]{:S(2)}) %all-to-all-start) | async-done | bytes 1048608 | tf_op jit(solution)/shard_map/all_to_all | solution.py:93
  35.6 0.0 collective-permute-done.1.refs_4_
  35.6 0.0 copy-done
  35.7 4.2 %shard_map.47 = bf16[8,128,128]{2,1,0:T(8,128)(2,1)} custom-call(s32[8,8]{1,0:T(8,128)S(1)} %copy-done.1, s32[8,8]{1,0:T(8,128)S(1)} %collective-permute-done.refs_1_, bf16[32,128,128]{2,1,0:T(8,128)(2,1)S(1)} %all-to-all-done.refs_2_, bf16[8,8,128,128]{3,2,1,0:T(8,128)(2,1)S(1)} %copy-done, bf16[8,8,128,128]{3,2,1,0:T(8,128)(2,1)} %collective-permute-done.1.refs_4_), custom_call_target="tpu_custom_call" | custom-call | tf_op jit(solution)/shard_map/pallas_call | solution.py:96
Async XLA Ops:
  0.0 10.8 %copy-start.1 = (s32[8,8]{1,0:T(8,128)S(1)}, s32[8,8]{1,0:T(8,128)}, u32[]{:S(2)}) copy-start(s32[8,8]{1,0:T(8,128)} %refs_0_.1) | copy-start | bytes 772
  0.0 35.6 %collective-permute-start.1 = (bf16[8,8,128,128]{3,2,1,0:T(8,128)(2,1)}, bf16[8,8,128,128]{3,2,1,0:T(8,128)(2,1)}, u32[]{:S(2)}, u32[]{:S(2)}) collective-permute-start(bf16[8,8,128,128]{3,2,1,0:T(8,128)(2,1)} %refs_3_.1), channel_id=1, source_target_pairs={{0,1},{1,0},{2,3},{3,2},{4,5},{5,4},{6,7},{7,6},{8,9},{9,8},{10,11... | collective-permute-start | bytes 6291464 | tf_op jit(solution)/shard_map/ppermute | solution.py:89
  2.8 32.9 %copy-start = (bf16[8,8,128,128]{3,2,1,0:T(8,128)(2,1)S(1)}, bf16[8,8,128,128]{3,2,1,0:T(8,128)(2,1)}, u32[]{:S(2)}) copy-start(bf16[8,8,128,128]{3,2,1,0:T(8,128)(2,1)} %refs_3_.1) | copy-start | bytes 6291460
  2.8 32.8 %all-to-all-start = ((bf16[32,128,128]{2,1,0:T(8,128)(2,1)}), bf16[32,128,128]{2,1,0:T(8,128)(2,1)S(1)}, u32[]{:S(2)}, u32[]{:S(2)}) async-start(bf16[32,128,128]{2,1,0:T(8,128)(2,1)} %shard_map.46), calls=%async_computation | async-start | bytes 2097152 | tf_op jit(solution)/shard_map/all_to_all | solution.py:93
  10.8 1.2 %collective-permute-start = (s32[8,8]{1,0:T(8,128)S(1)}, s32[8,8]{1,0:T(8,128)S(1)}, u32[]{:S(2)}, u32[]{:S(2)}) collective-permute-start(s32[8,8]{1,0:T(8,128)S(1)} %copy-done.1), channel_id=1, source_target_pairs={{0,1},{1,0},{2,3},{3,2},{4,5},{5,4},{6,7},{7,6},{8,9},{9,8},{10,11... | collective-permute-start | bytes 776 | tf_op jit(solution)/shard_map/ppermute | solution.py:88
